TPU v7x, 512 devices: a whole 4x8x8 slice. The times are simulated.
512 devices in a mesh: inst: 32 (over x, z), head: 16 (over y, core).
Axes of the slice: x: 4, y: 8, z: 8, core: 2. Of those that a mesh axis runs over, the one named last changes fastest.
Arguments:
- hidden_rows: bfloat16 [32, 32, 16, 9216], P('inst', None, None, 'head'), may hold values from -6 to 6
- send_counts: int32 [32, 32], P('inst'), may hold values from 0 to 16, as said below
- row_session: int32 [32, 32, 16], P('inst'), may hold values from 0 to 1, as said below
- row_position: int32 [32, 32, 16], P('inst'), may hold values from 0 to 1023, as said below
- resident_lengths: int32 [64], P('inst'), may hold values from 1 to 512, as said below
- kv_weight: bfloat16 [9216, 12288], P('inst', 'head'), may hold values from -0.0625 to 0.0625
- key_cache: bfloat16 [64, 1024, 6144], P('inst', None, 'head'), as said below
- value_cache: bfloat16 [64, 1024, 6144], P('inst', None, 'head'), may hold values from -6 to 6
- query: bfloat16 [64, 6144], P('inst', 'head'), as said below
- new_key: bfloat16 [64, 6144], P('inst', 'head'), may hold values from -6 to 6
- new_value: bfloat16 [64, 6144], P('inst', 'head'), may hold values from -6 to 6
Outputs:
- attended: bfloat16 [64, 6144], P('inst', 'head')
Inputs may be any that keep to these rules, and one draw needn't show every extreme that they name: `send_counts`: at most 16 live slots from one source to one destination; in every draw one destination instance receives 16 rows from every source. `row_session`: for a live slot, a session of the destination instance; 0 in slots that are not live. The destination that receives 16 rows from every source sends all of them to one of its sessions. `row_position`: the live rows of one destination session take each of the positions from its resident length to its resident length plus their number minus 1 exactly once; 0 in slots that are not live. In every draw some session's rows end at position 1023. `resident_lengths`: A session's resident length plus its restored rows stays within 1024 positions. `key_cache`: entries of order one. `query`: entries of order one or a few tens.
All inputs are finite; a program needn't handle non-finite values.
Results may differ from a plain program's by a relative error of at most 0.009.
Values may be sent and summed in bfloat16 or wider, within the bound.
No kernel may reach another device: no remote copies, remote signals or barrier semaphores. Data moves between devices by JAX's collectives and lax.ppermute only.
A program may use at most 192 MiB of HBM per device.

v0:
```python
import math
import jax
import jax.numpy as jnp
from jax import lax
from jax.sharding import PartitionSpec as P

HDIM = 128
masked_score = -1e30


def local(
    hidden_rows,
    send_counts,
    row_session,
    row_position,
    resident_lengths,
    kv_weight,
    key_cache,
    value_cache,
    query,
    new_key,
    new_value,
):
    sources = hidden_rows.shape[1]
    slot_cap = hidden_rows.shape[2]
    slot_count = sources * slot_cap
    head_dev = query.shape[1] // HDIM
    sessions_dev = key_cache.shape[0]
    context = key_cache.shape[1]
    inverse_root = 1.0 / math.sqrt(HDIM)
    arrived, counts_in, session_in, position_in = (
        lax.all_to_all(hidden_rows, "inst", split_axis=1, concat_axis=0, tiled=True),
        lax.all_to_all(send_counts, "inst", split_axis=1, concat_axis=0, tiled=True),
        lax.all_to_all(row_session, "inst", split_axis=1, concat_axis=0, tiled=True),
        lax.all_to_all(row_position, "inst", split_axis=1, concat_axis=0, tiled=True),
    )
    full_rows = lax.all_gather(
        arrived.reshape(slot_count, arrived.shape[3]), "head", axis=1, tiled=True
    )
    restored = jnp.dot(
        full_rows,
        lax.all_gather(kv_weight, "inst", axis=0, tiled=True),
        preferred_element_type=jnp.float32,
    )
    restored = restored.astype(jnp.bfloat16).reshape(slot_count, head_dev, 2, HDIM)
    restored_keys = restored[:, :, 0]
    restored_values = restored[:, :, 1]
    slot_live = (jnp.arange(slot_cap)[None, :] < counts_in).reshape(slot_count)
    session_map = session_in.reshape(slot_count)
    position_map = position_in.reshape(slot_count)
    member = (session_map[None, :] == jnp.arange(sessions_dev)[:, None]) & slot_live[None, :]
    queries = query.reshape(sessions_dev, head_dev, HDIM)
    cache_keys = key_cache.reshape(sessions_dev, context, head_dev, HDIM)
    cache_values = value_cache.reshape(sessions_dev, context, head_dev, HDIM)
    own_score = (
        jnp.sum(
            queries.astype(jnp.float32)
            * new_key.reshape(sessions_dev, head_dev, HDIM).astype(jnp.float32),
            axis=-1,
        )
        * inverse_root
    )
    fresh_value = new_value.reshape(sessions_dev, head_dev, HDIM).astype(jnp.float32)
    position_ids = jnp.arange(context)
    target = jnp.where(slot_live, position_map, context)
    key_rows = cache_keys.at[session_map, target].set(restored_keys, mode="drop")
    value_rows = cache_values.at[session_map, target].set(restored_values, mode="drop")
    totals = resident_lengths + jnp.sum(member.astype(jnp.int32), axis=1)
    scores = (
        jnp.einsum("shd,sphd->shp", queries, key_rows, preferred_element_type=jnp.float32)
        * inverse_root
    )
    scores = jnp.where((position_ids[None, :] < totals[:, None])[:, None, :], scores, masked_score)
    highest = jnp.maximum(jnp.max(scores, axis=-1), own_score)
    weights = jnp.exp(scores - highest[:, :, None])
    own_weight = jnp.exp(own_score - highest)
    denominator = jnp.sum(weights, axis=-1) + own_weight
    probability = (weights / denominator[:, :, None]).astype(jnp.bfloat16)
    attended = jnp.einsum(
        "shp,sphd->shd", probability, value_rows, preferred_element_type=jnp.float32
    )
    own_prob = (own_weight / denominator).astype(jnp.bfloat16)
    attended = attended + own_prob.astype(jnp.float32)[:, :, None] * fresh_value
    return attended.astype(jnp.bfloat16).reshape(sessions_dev, head_dev * HDIM)


def solution(mesh):
    placed = (
        P("inst", None, None, "head"),
        P("inst", None),
        P("inst", None, None),
        P("inst", None, None),
        P("inst"),
        P("inst", "head"),
        P("inst", None, "head"),
        P("inst", None, "head"),
        P("inst", "head"),
        P("inst", "head"),
        P("inst", "head"),
    )
    return jax.shard_map(
        local, mesh=mesh, in_specs=placed, out_specs=P("inst", "head"), check_vma=False
    )
```

profile of v0, /device:TPU:1, one launch (start us, length us, event | category | flops | bytes accessed | tf_op | source)
XLA Modules:
  0.0 339.8 jit_solution(13822352009684851430)
XLA Ops:
  6.6 30.2 %all_to_all.40 = bf16[1,32,16,576]{3,2,0,1:T(8,128)(2,1)S(1)} all-to-all(bf16[1,32,16,576]{3,2,0,1:T(8,128)(2,1)} %bitcast.46), channel_id=1, replica_groups=mesh['inst'=32,'head'=16] {'inst'}, dimensions={1} | all-to-all | bytes 1179648 | tf_op jit(solution)/shard_map/all_to_all | solution.py:32
  36.9 1.1 copy.77
  38.0 0.7 all-gather.5.cloned.1.call-update
  38.7 0.7 copy.73
  39.4 8.4 %all-to-all-start.1 = ((s32[1,32,1]{2,0,1:T(1,128)}), s32[1,32,1]{2,0,1:T(1,128)S(1)}, u32[]{:S(2)}, u32[]{:S(2)}) async-start(s32[1,32,1]{2,0,1:T(1,128)} %copy.73), calls=%async_computation.1 | async-start | bytes 32768 | tf_op jit(solution)/shard_map/all_to_all | solution.py:33
  47.9 0.7 copy.72
  48.5 7.9 %all-to-all-done.1 = s32[1,32,1]{2,0,1:T(1,128)S(1)} async-done(((s32[1,32,1]{2,0,1:T(1,128)}), s32[1,32,1]{2,0,1:T(1,128)S(1)}, u32[]{:S(2)}, u32[]{:S(2)}) %all-to-all-start.1) | async-done | bytes 160 | tf_op jit(solution)/shard_map/all_to_all | solution.py:33
  56.4 3.8 %all-to-all-start = ((s32[1,32,16]{2,0,1:T(1,128)}), s32[1,32,16]{2,0,1:T(1,128)S(1)}, u32[]{:S(2)}, u32[]{:S(2)}) async-start(s32[1,32,16]{2,0,1:T(1,128)} %copy.72), calls=%async_computation | async-start | bytes 32768 | tf_op jit(solution)/shard_map/all_to_all | solution.py:34
  60.4 0.7 copy.75
  61.1 0.7 copy.74
  61.9 2.6 copy.79
  64.5 0.7 copy.82
  65.3 2.6 copy.84
  67.9 0.7 reduce.1
  68.5 0.3 all-to-all-done
  68.8 9.1 %all-to-all-start.2 = ((s32[1,32,16]{2,0,1:T(1,128)}), s32[1,32,16]{2,0,1:T(1,128)S(1)}, u32[]{:S(2)}, u32[]{:S(2)}) async-start(s32[1,32,16]{2,0,1:T(1,128)} %copy.75), calls=%async_computation.2 | async-start | bytes 32768 | tf_op jit(solution)/shard_map/all_to_all | solution.py:35
  78.3 0.5 broadcast.131
  78.8 0.7 reduce.10
  79.6 6.8 %all-to-all-done.2 = s32[1,32,16]{2,0,1:T(1,128)S(1)} async-done(((s32[1,32,16]{2,0,1:T(1,128)}), s32[1,32,16]{2,0,1:T(1,128)S(1)}, u32[]{:S(2)}, u32[]{:S(2)}) %all-to-all-start.2) | async-done | bytes 2080 | tf_op jit(solution)/shard_map/all_to_all | solution.py:35
  86.4 0.7 reduce.9
  87.4 15.0 %all-gather.3.cloned.1.call-done = bf16[512,9216]{0,1:T(8,128)(2,1)} async-done(((bf16[512,576]{0,1:T(8,128)(2,1)}), bf16[512,9216]{0,1:T(8,128)(2,1)}) %all-gather.3.cloned.1.call-update) | async-done | bytes 9437200 | tf_op jit(solution)/shard_map/all_gather | solution.py:37
  102.4 135.1 %all-gather.5.cloned.1.call-done = bf16[9216,768]{1,0:T(8,128)(2,1)} async-done(((bf16[288,768]{1,0:T(8,128)(2,1)}), bf16[9216,768]{1,0:T(8,128)(2,1)}) %all-gather.5.cloned.1.call-update) | async-done | bytes 14155792 | tf_op jit(solution)/shard_map/all_gather | solution.py:42
  237.4 14.2 %convolution_convert_fusion = bf16[512,768]{1,0:T(8,128)(2,1)S(1)} fusion(bf16[512,9216]{0,1:T(8,128)(2,1)} %all-gather.3.cloned.1.call-done, bf16[9216,768]{1,0:T(8,128)(2,1)} %all-gather.5.cloned.1.call-done), kind=kOutput, calls=%fused_computation.6 | convolution fusion | flops 7248150528 | bytes 24379392 | tf_op jit(solution)/shard_map/dot_general | solution.py:40
  251.6 0.2 reshape.179
  251.8 1.1 fusion.15
  253.1 0.3 copy.85
  253.4 0.3 copy.80
  253.8 55.4 %scatter_fusion = bf16[2,1024,3,128]{3,2,1,0:T(4,128)(2,1)} fusion(bf16[2,1024,3,128]{3,2,1,0:T(4,128)(2,1)} %copy.79, s32[512]{0:T(512)S(1)} %bitcast.41, bf16[512,3,128]{2,1,0:T(4,128)(2,1)S(1)} %copy.80), kind=kCustom, calls=%fused_computation | custom fusion | bytes 1183744 | tf_op jit(solution)/shard_map/scatter | solution.py:66
  309.2 2.1 fusion.2
  311.8 20.1 %scatter_fusion.1 = bf16[2,1024,3,128]{3,2,1,0:T(4,128)(2,1)S(1)} fusion(bf16[2,1024,3,128]{3,2,1,0:T(4,128)(2,1)S(1)} %copy-done, s32[512]{0:T(512)S(1)} %bitcast.42, bf16[512,3,128]{2,1,0:T(4,128)(2,1)S(1)} %copy.85), kind=kCustom, calls=%fused_computation.1 | custom fusion | bytes 1183744 | tf_op jit(solution)/shard_map/scatter | solution.py:67
  331.9 0.4 fusion
  332.3 0.6 copy.115
  (47 shorter events, 1.8 us)
Async XLA Ops:
  6.5 32.2 %copy-start.8 = (s32[1,32]{1,0:T(1,128)S(1)}, s32[1,32]{1,0:T(1,128)}, u32[]{:S(2)}) copy-start(s32[1,32]{1,0:T(1,128)} %param.12) | copy-start | bytes 388
  6.5 41.3 %copy-start.5 = (bf16[2,384]{1,0:T(2,128)(2,1)S(1)}, bf16[2,384]{1,0:T(2,128)(2,1)}, u32[]{:S(2)}) copy-start(bf16[2,384]{1,0:T(2,128)(2,1)} %param.19) | copy-start | bytes 4612
  6.5 41.3 %copy-start.6 = (bf16[2,384]{1,0:T(2,128)(2,1)S(1)}, bf16[2,384]{1,0:T(2,128)(2,1)}, u32[]{:S(2)}) copy-start(bf16[2,384]{1,0:T(2,128)(2,1)} %param.20) | copy-start | bytes 4612
  6.5 41.3 %copy-start.3 = (s32[1,32,16]{1,2,0:T(8,128)S(1)}, s32[1,32,16]{1,2,0:T(8,128)}, u32[]{:S(2)}) copy-start(s32[1,32,16]{1,2,0:T(8,128)} %param.13) | copy-start | bytes 6148
  6.5 53.9 %copy-start.7 = (bf16[2,384]{1,0:T(2,128)(2,1)S(1)}, bf16[2,384]{1,0:T(2,128)(2,1)}, u32[]{:S(2)}) copy-start(bf16[2,384]{1,0:T(2,128)(2,1)} %param.21) | copy-start | bytes 4612
  6.5 53.9 %copy-start.4 = (s32[1,32,16]{1,2,0:T(8,128)S(1)}, s32[1,32,16]{1,2,0:T(8,128)}, u32[]{:S(2)}) copy-start(s32[1,32,16]{1,2,0:T(8,128)} %param.14) | copy-start | bytes 6148
  6.6 54.5 %copy-start.1 = (bf16[2,1024,384]{2,1,0:T(8,128)(2,1)S(1)}, bf16[2,1024,384]{2,1,0:T(8,128)(2,1)}, u32[]{:S(2)}) copy-start(bf16[2,1024,384]{2,1,0:T(8,128)(2,1)} %param.17) | copy-start | bytes 4718596
  6.6 95.8 %all-gather.3.cloned.1.call-start = ((), (), s32[]{:S(2)}) async-start(), calls=%async_computation.4 | async-start | bytes 10027008 | tf_op jit(solution)/shard_map/all_gather | solution.py:37
  37.9 199.5 %all-gather.5.cloned.1.call-start = ((), (), s32[]{:S(2)}) async-start(), calls=%async_computation.5 | async-start | bytes 14598144 | tf_op jit(solution)/shard_map/all_gather | solution.py:42
  39.4 17.0 %all-to-all-start.1 = ((s32[1,32,1]{2,0,1:T(1,128)}), s32[1,32,1]{2,0,1:T(1,128)S(1)}, u32[]{:S(2)}, u32[]{:S(2)}) async-start(s32[1,32,1]{2,0,1:T(1,128)} %copy.73), calls=%async_computation.1 | async-start | bytes 32768 | tf_op jit(solution)/shard_map/all_to_all | solution.py:33
  56.4 12.4 %all-to-all-start = ((s32[1,32,16]{2,0,1:T(1,128)}), s32[1,32,16]{2,0,1:T(1,128)S(1)}, u32[]{:S(2)}, u32[]{:S(2)}) async-start(s32[1,32,16]{2,0,1:T(1,128)} %copy.72), calls=%async_computation | async-start | bytes 32768 | tf_op jit(solution)/shard_map/all_to_all | solution.py:34
  61.9 2.6 copy-start.2
  65.3 22.0 %copy-start.9 = (s32[2]{0:T(128)S(1)}, s32[2]{0:T(128)}, u32[]{:S(2)}) copy-start(s32[2]{0:T(128)} %param.15) | copy-start | bytes 28
  68.8 17.6 %all-to-all-start.2 = ((s32[1,32,16]{2,0,1:T(1,128)}), s32[1,32,16]{2,0,1:T(1,128)S(1)}, u32[]{:S(2)}, u32[]{:S(2)}) async-start(s32[1,32,16]{2,0,1:T(1,128)} %copy.75), calls=%async_computation.2 | async-start | bytes 32768 | tf_op jit(solution)/shard_map/all_to_all | solution.py:35
  253.8 58.1 %copy-start = (bf16[2,1024,3,128]{3,2,1,0:T(4,128)(2,1)S(1)}, bf16[2,1024,3,128]{3,2,1,0:T(4,128)(2,1)}, u32[]{:S(2)}) copy-start(bf16[2,1024,3,128]{3,2,1,0:T(4,128)(2,1)} %copy.84) | copy-start | bytes 4718596
Sparse Core Ops, SparseCore 0:
  38.1 64.2 all-gather.2
  105.5 131.8 all-gather.4
where the time goes:
time: 341 us; the launch traced here: 340 us
  waiting for transfers between devices  166 us (49%)
  local copies, waits for them, and re-layouts  89.2 us (26%)
  blocking collectives  30.2 us (9%)
  starting transfers between devices  21.4 us (6%)
  matrix products  16.6 us (5%)
  between operations  13.6 us (4%)
    all_gather x1, waiting for transfers between devices, local(): lax.all_gather(kv_weight, 'inst', axis=0, tiled=True)  135 us
    scatter x1, local copies, waits for them, and re-layouts, local(): cache_keys.at[session_map, target].set(restored_keys, mode='drop')  55.4 us
    all_to_all x1, blocking collectives, local(): lax.all_to_all(hidden_rows, 'inst', split_axis=1, concat_axis=0, tiled=True)  30.2 us
    scatter x1, local copies, waits for them, and re-layouts, local(): cache_values.at[session_map, target].set(restored_values, mode='drop')  20.1 us
    all_gather x1, waiting for transfers between devices, local(): lax.all_gather(arrived.reshape(slot_count, arrived.shape[3]), 'head', axi...  15 us
    dot_general x1, matrix products, local(): jnp.dot(full_rows, lax.all_gather(kv_weight, 'inst', axis=0, tiled=True),...  14.2 us
    all_to_all x1, starting transfers between devices, local(): lax.all_to_all(row_position, 'inst', split_axis=1, concat_axis=0, tiled=T...  9.1 us
    all_to_all x1, starting transfers between devices, local(): lax.all_to_all(send_counts, 'inst', split_axis=1, concat_axis=0, tiled=True)  8.39 us
  transfers between devices with their start and end apart: 5, of which 5 were waited for; matrix products, arithmetic and copies ran while one was open for 4% of the time, Pallas kernels for 0%

commit v1 on v0

--- a/solution.py
+++ b/solution.py
@@ -39,7 +39,9 @@
     )
     restored = jnp.dot(
         full_rows,
-        lax.all_gather(kv_weight, "inst", axis=0, tiled=True),
+        jnp.concatenate(
+            lax.all_to_all(jnp.stack([kv_weight] * lax.axis_size("inst")), "inst", 0, 0), axis=0
+        ),
         preferred_element_type=jnp.float32,
     )
     restored = restored.astype(jnp.bfloat16).reshape(slot_count, head_dev, 2, HDIM)

time: 341 us -> 499 us (1.46)
  waiting for transfers between devices: 166 us -> 313 us
    all_to_all x1, waiting for transfers between devices: 0.32 us -> 237 us  [local(): lax.all_to_all(jnp.stack([kv_weight] * lax.axis_size('inst')), 'inst', 0, 0)]
    all_gather x1 -> x0, waiting for transfers between devices: 135 us -> none  [local(): lax.all_gather(kv_weight, 'inst', axis=0, tiled=True)]
    all_gather x1, waiting for transfers between devices: 15 us -> 61.2 us  [local(): lax.all_gather(arrived.reshape(slot_count, arrived.shape[3]), 'head', axi...]
    all_to_all x1, blocking collectives: 30.2 us -> 17.8 us  [local(): lax.all_to_all(hidden_rows, 'inst', split_axis=1, concat_axis=0, tiled=True)]
    all_to_all x0 -> x1, blocking collectives: none -> 11.6 us  [local(): lax.all_to_all(row_session, 'inst', split_axis=1, concat_axis=0, tiled=True)]
    another operation x0 -> x1, local copies, waits for them, and re-layouts: none -> 7.74 us  [local(): jnp.stack([kv_weight] * lax.axis_size('inst'))]
    all_to_all x1, starting transfers between devices: 9.1 us -> 3.77 us  [local(): lax.all_to_all(row_position, 'inst', split_axis=1, concat_axis=0, tiled=T...]
    all_to_all x1, starting transfers between devices: 8.39 us -> 13.7 us  [local(): lax.all_to_all(send_counts, 'inst', split_axis=1, concat_axis=0, tiled=True)]
  transfers between devices with their start and end apart: 5 -> 4, of which waited for: 5 -> 4; matrix products, arithmetic and copies ran while one was open for 4% -> 3% of each run, Pallas kernels for 0% -> 0%
where the time goes in v1:
time: 499 us; the launch traced here: 494 us
  waiting for transfers between devices  313 us (63%)
  local copies, waits for them, and re-layouts  93.7 us (19%)
  blocking collectives  29.4 us (6%)
  starting transfers between devices  24.6 us (5%)
  matrix products  16.6 us (3%)
  between operations  13.6 us (3%)
    all_to_all x1, waiting for transfers between devices, local(): lax.all_to_all(jnp.stack([kv_weight] * lax.axis_size('inst')), 'inst', 0, 0)  237 us
    all_gather x1, waiting for transfers between devices, local(): lax.all_gather(arrived.reshape(slot_count, arrived.shape[3]), 'head', axi...  61.2 us
    scatter x1, local copies, waits for them, and re-layouts, local(): cache_keys.at[session_map, target].set(restored_keys, mode='drop')  51.1 us
    scatter x1, local copies, waits for them, and re-layouts, local(): cache_values.at[session_map, target].set(restored_values, mode='drop')  19.8 us
    all_to_all x1, blocking collectives, local(): lax.all_to_all(hidden_rows, 'inst', split_axis=1, concat_axis=0, tiled=True)  17.8 us
    dot_general x1, matrix products, local(): jnp.dot(full_rows, jnp.concatenate(lax.all_to_all(jnp.stack([kv_weight] *...  14.2 us
    all_to_all x1, starting transfers between devices, local(): lax.all_to_all(send_counts, 'inst', split_axis=1, concat_axis=0, tiled=True)  13.7 us
    all_to_all x1, blocking collectives, local(): lax.all_to_all(row_session, 'inst', split_axis=1, concat_axis=0, tiled=True)  11.6 us
  transfers between devices with their start and end apart: 4, of which 4 were waited for; matrix products, arithmetic and copies ran while one was open for 3% of the time, Pallas kernels for 0%

profile of v1, /device:TPU:1, one launch (start us, length us, event | category | flops | bytes accessed | tf_op | source)
XLA Modules:
  0.0 494.3 jit_solution(8871331640317069051)
XLA Ops:
  6.5 1.3 copy.73
  7.9 13.7 %all-to-all-start.1 = ((s32[1,32,1]{2,0,1:T(1,128)}), s32[1,32,1]{2,0,1:T(1,128)S(1)}, u32[]{:S(2)}, u32[]{:S(2)}) async-start(s32[1,32,1]{2,0,1:T(1,128)} %copy.73), calls=%async_computation.1 | async-start | bytes 32768 | tf_op jit(solution)/shard_map/all_to_all | solution.py:33
  21.6 1.4 copy.75
  23.0 7.2 %all-to-all-done.1 = s32[1,32,1]{2,0,1:T(1,128)S(1)} async-done(((s32[1,32,1]{2,0,1:T(1,128)}), s32[1,32,1]{2,0,1:T(1,128)S(1)}, u32[]{:S(2)}, u32[]{:S(2)}) %all-to-all-start.1) | async-done | bytes 160 | tf_op jit(solution)/shard_map/all_to_all | solution.py:33
  30.2 3.8 all-to-all-start.2
  34.0 0.8 copy.72
  34.8 7.9 %all-to-all-done.2 = s32[1,32,16]{2,0,1:T(1,128)S(1)} async-done(((s32[1,32,16]{2,0,1:T(1,128)}), s32[1,32,16]{2,0,1:T(1,128)S(1)}, u32[]{:S(2)}, u32[]{:S(2)}) %all-to-all-start.2) | async-done | bytes 2080 | tf_op jit(solution)/shard_map/all_to_all | solution.py:35
  42.6 11.6 %all_to_all.45 = s32[1,32,16]{2,0,1:T(1,128)S(1)} all-to-all(s32[1,32,16]{2,0,1:T(1,128)S(1)} %copy.72), channel_id=1, replica_groups=mesh['inst'=32,'head'=16] {'inst'}, dimensions={1} | all-to-all | bytes 4096 | tf_op jit(solution)/shard_map/all_to_all | solution.py:34
  54.2 17.8 %all_to_all.46 = bf16[1,32,16,576]{3,2,0,1:T(8,128)(2,1)S(1)} all-to-all(bf16[1,32,16,576]{3,2,0,1:T(8,128)(2,1)} %bitcast.45), channel_id=1, replica_groups=mesh['inst'=32,'head'=16] {'inst'}, dimensions={1} | all-to-all | bytes 1179648 | tf_op jit(solution)/shard_map/all_to_all | solution.py:32
  72.1 7.7 %stack.2 = bf16[32,288,768]{2,1,0:T(8,128)(2,1)} broadcast(bf16[288,768]{1,0:T(8,128)(2,1)} %param.16), dimensions={1,2} | broadcast | bytes 14598144 | tf_op jit(solution)/shard_map/stack | solution.py:43
  79.8 6.9 %all-to-all-start.4 = ((bf16[32,288,768]{2,1,0:T(8,128)(2,1)}), bf16[32,288,768]{2,1,0:T(8,128)(2,1)}, u32[]{:S(2)}, u32[]{:S(2)}) async-start(bf16[32,288,768]{2,1,0:T(8,128)(2,1)} %stack.2), calls=%async_computation.4 | async-start | bytes 28311552 | tf_op jit(solution)/shard_map/all_to_all | solution.py:43
  86.7 0.2 all-gather.2.cloned.1.call-start
  86.9 1.1 copy.77
  88.1 0.7 copy.74
  88.9 2.6 copy.79
  91.6 0.8 copy.82
  92.4 2.5 copy.84
  95.0 0.7 reduce.1
  95.9 0.5 broadcast.133
  96.4 0.7 reduce.9
  97.3 0.7 reduce.10
  98.3 61.2 %all-gather.2.cloned.1.call-done = bf16[512,9216]{0,1:T(8,128)(2,1)} async-done(((bf16[512,576]{0,1:T(8,128)(2,1)}), bf16[512,9216]{0,1:T(8,128)(2,1)}) %all-gather.2.cloned.1.call-update) | async-done | bytes 9437200 | tf_op jit(solution)/shard_map/all_gather | solution.py:37
  159.5 237.1 %all-to-all-done.4 = bf16[32,288,768]{2,1,0:T(8,128)(2,1)} async-done(((bf16[32,288,768]{2,1,0:T(8,128)(2,1)}), bf16[32,288,768]{2,1,0:T(8,128)(2,1)}, u32[]{:S(2)}, u32[]{:S(2)}) %all-to-all-start.4) | async-done | bytes 14155808 | tf_op jit(solution)/shard_map/all_to_all | solution.py:43
  396.6 14.2 %convolution_convert_fusion = bf16[512,768]{1,0:T(8,128)(2,1)S(1)} fusion(bf16[512,9216]{0,1:T(8,128)(2,1)} %all-gather.2.cloned.1.call-done, bf16[9216,768]{1,0:T(8,128)(2,1)} %bitcast.5), kind=kOutput, calls=%fused_computation.6 | convolution fusion | flops 7248150528 | bytes 24379392 | tf_op jit(solution)/shard_map/dot_general | solution.py:40
  411.0 1.1 fusion.15
  412.2 0.3 copy.80
  412.6 51.1 %scatter_fusion = bf16[2,1024,3,128]{3,2,1,0:T(4,128)(2,1)} fusion(bf16[2,1024,3,128]{3,2,1,0:T(4,128)(2,1)} %copy.79, s32[512]{0:T(512)S(1)} %bitcast.40, bf16[512,3,128]{2,1,0:T(4,128)(2,1)S(1)} %copy.80), kind=kCustom, calls=%fused_computation | custom fusion | bytes 1183744 | tf_op jit(solution)/shard_map/scatter | solution.py:68
  463.6 2.1 fusion.2
  466.2 0.3 copy.85
  466.6 19.8 %scatter_fusion.1 = bf16[2,1024,3,128]{3,2,1,0:T(4,128)(2,1)S(1)} fusion(bf16[2,1024,3,128]{3,2,1,0:T(4,128)(2,1)S(1)} %copy-done, s32[512]{0:T(512)S(1)} %bitcast.41, bf16[512,3,128]{2,1,0:T(4,128)(2,1)S(1)} %copy.85), kind=kCustom, calls=%fused_computation.1 | custom fusion | bytes 1183744 | tf_op jit(solution)/shard_map/scatter | solution.py:69
  486.4 0.4 fusion
  486.9 0.6 copy.115
  (40 shorter events, 1.9 us)
Async XLA Ops:
  7.9 22.3 %all-to-all-start.1 = ((s32[1,32,1]{2,0,1:T(1,128)}), s32[1,32,1]{2,0,1:T(1,128)S(1)}, u32[]{:S(2)}, u32[]{:S(2)}) async-start(s32[1,32,1]{2,0,1:T(1,128)} %copy.73), calls=%async_computation.1 | async-start | bytes 32768 | tf_op jit(solution)/shard_map/all_to_all | solution.py:33
  30.2 12.4 %all-to-all-start.2 = ((s32[1,32,16]{2,0,1:T(1,128)}), s32[1,32,16]{2,0,1:T(1,128)S(1)}, u32[]{:S(2)}, u32[]{:S(2)}) async-start(s32[1,32,16]{2,0,1:T(1,128)} %copy.75), calls=%async_computation.2 | async-start | bytes 32768 | tf_op jit(solution)/shard_map/all_to_all | solution.py:35
  79.8 8.2 %copy-start.3 = (bf16[2,384]{1,0:T(2,128)(2,1)S(1)}, bf16[2,384]{1,0:T(2,128)(2,1)}, u32[]{:S(2)}) copy-start(bf16[2,384]{1,0:T(2,128)(2,1)} %param.19) | copy-start | bytes 4612
  79.8 316.8 %all-to-all-start.4 = ((bf16[32,288,768]{2,1,0:T(8,128)(2,1)}), bf16[32,288,768]{2,1,0:T(8,128)(2,1)}, u32[]{:S(2)}, u32[]{:S(2)}) async-start(bf16[32,288,768]{2,1,0:T(8,128)(2,1)} %stack.2), calls=%async_computation.4 | async-start | bytes 28311552 | tf_op jit(solution)/shard_map/all_to_all | solution.py:43
  86.7 1.4 copy-start.1
  86.7 72.8 %all-gather.2.cloned.1.call-start = ((), (), s32[]{:S(2)}) async-start(), calls=%async_computation.5 | async-start | bytes 10027008 | tf_op jit(solution)/shard_map/all_gather | solution.py:37
  88.9 2.6 copy-start.4
  88.9 2.8 copy-start.2
  92.4 2.5 copy-start.5
  92.4 5.8 %copy-start.6 = (s32[2]{0:T(128)S(1)}, s32[2]{0:T(128)}, u32[]{:S(2)}) copy-start(s32[2]{0:T(128)} %param.15) | copy-start | bytes 28
  412.6 54.1 %copy-start = (bf16[2,1024,3,128]{3,2,1,0:T(4,128)(2,1)S(1)}, bf16[2,1024,3,128]{3,2,1,0:T(4,128)(2,1)}, u32[]{:S(2)}) copy-start(bf16[2,1024,3,128]{3,2,1,0:T(4,128)(2,1)} %copy.84) | copy-start | bytes 4718596
Sparse Core Ops, SparseCore 0:
  89.7 69.7 all-gather.1
